TPU v7x, 256 devices: a whole 4x4x8 slice. The times are simulated.
256 devices in a mesh: stretch: 32 (over y_lo, z, core), head: 8 (over y_hi, x).
Axes of the slice: x: 4, y: 4 (y_hi: 2, y_lo: 2; y = y_hi * 2 + y_lo), z: 8, core: 2. Of those that a mesh axis runs over, the one named last changes fastest.
Arguments:
- query_raw: bfloat16 [8192, 5120], P('stretch', 'head'), may hold values from -1000 to 1000
- key_raw: bfloat16 [8192, 5120], P('stretch', 'head'), may hold values from -1000 to 1000
- values: bfloat16 [8192, 5120], P('stretch', 'head'), may hold values from -6 to 6
- query_gain: float32 [5120], P('head'), may hold values from 0.25 to 1.75
- key_gain: float32 [5120], P('head'), may hold values from 0.25 to 1.75
- recent_ids: int32 [32, 2], P('stretch'), may hold values from -1 to 30, as said below
- sink_ids: int32 [32, 1], P('stretch'), may hold values from -1 to 1, as said below
- out_grad: bfloat16 [8192, 5120], P('stretch', 'head'), may hold values from -6 to 6
Outputs:
- attended: bfloat16 [8192, 5120], P('stretch', 'head')
- query_grad: bfloat16 [8192, 5120], P('stretch', 'head')
- key_grad: bfloat16 [8192, 5120], P('stretch', 'head')
- value_grad: bfloat16 [8192, 5120], P('stretch', 'head')
Inputs may be any that keep to these rules, and one draw needn't show every extreme that they name: `recent_ids`: row c names the stretch c - 1 first and then one stretch from c - 3 to c - 2; an entry that would lie before stretch 0 is -1. `sink_ids`: row c names one stretch among the first 2 that lies before c, or -1 where none does; it may also stand in the row's recent list. Row c names stretch c - 1 for c from 1 to 2, and the last row names stretch 1.
All inputs are finite; a program needn't handle non-finite values.
Results may differ from a plain program's by a relative error of at most 0.04.
Values may be sent and summed in bfloat16 or wider, within the bound.
A program may use at most 64 MiB of HBM per device.

v0:
```python
from functools import reduce

import jax
import jax.numpy as jnp
from jax import lax
from jax.sharding import PartitionSpec as P

D = 5120
HDIM = 128
WINDOW = 3
SINK_POOL = 2


EPS = 1e-06


def shifted_2(x, axis, by):
    devices = lax.axis_size(axis)
    pairs = [(i, i + by) for i in range(devices) if 0 <= i + by < devices]
    return lax.ppermute(x, axis, pairs)


def broadcast(value, axis, source):
    kept = jnp.where(lax.axis_index(axis) == source, value, 0).astype(value.dtype)
    return lax.psum(kept, axis)


def block_scores(queries, keys, scale):
    return jnp.einsum("qhd,khd->hqk", queries, keys, preferred_element_type=jnp.float32) * scale


def key_terms(dscore, weight, queries, grads, scale):
    key_part = (
        jnp.einsum("hqk,qhd->khd", dscore, queries, preferred_element_type=jnp.float32) * scale
    )
    value_part = jnp.einsum("hqk,qhd->khd", weight, grads, preferred_element_type=jnp.float32)
    return (key_part, value_part)


def per_device(query_raw, key_raw, values, query_gain, key_gain, recent_ids, sink_ids, out_grad):
    rows, width = query_raw.shape
    heads = width // HDIM
    scale = HDIM ** (-0.5)
    position = lax.axis_index("stretch")
    query_float = query_raw.astype(jnp.float32)
    key_float = key_raw.astype(jnp.float32)
    query_square, key_square = lax.psum(
        (jnp.sum(query_float * query_float, axis=1), jnp.sum(key_float * key_float, axis=1)), "head"
    )
    query_inv = lax.rsqrt(query_square / D + EPS)[:, None]
    key_inv = lax.rsqrt(key_square / D + EPS)[:, None]
    query_norm = (
        (query_float * query_inv * query_gain).astype(jnp.bfloat16).reshape(rows, heads, HDIM)
    )
    key_norm = (key_float * key_inv * key_gain).astype(jnp.bfloat16).reshape(rows, heads, HDIM)
    value_rows = values.reshape(rows, heads, HDIM)
    grad_rows = out_grad.reshape(rows, heads, HDIM)
    far_id = recent_ids[0, 1]
    sink_id = sink_ids[0, 0]
    shifted = []
    for offset in range(1, WINDOW + 1):
        shifted.append(shifted_2((key_norm, value_rows), "stretch", offset))
    near_keys, near_values = shifted[0]
    far_keys, far_values = shifted[WINDOW - 1]
    offset = 2
    pick = far_id == position - offset
    far_keys = jnp.where(pick, shifted[offset - 1][0], far_keys)
    far_values = jnp.where(pick, shifted[offset - 1][1], far_values)
    sink_keys, sink_values = (None, None)
    for source in range(SINK_POOL):
        got_keys, got_values = (
            broadcast(key_norm, "stretch", source),
            broadcast(value_rows, "stretch", source),
        )
        if source == 0:
            sink_keys, sink_values = (got_keys, got_values)
        else:
            pick = sink_id == source
            sink_keys = jnp.where(pick, got_keys, sink_keys)
            sink_values = jnp.where(pick, got_values, sink_values)
    blocks = [
        (key_norm, value_rows, jnp.array(True)),
        (near_keys, near_values, position >= 1),
        (far_keys, far_values, far_id >= 0),
        (sink_keys, sink_values, sink_id >= 0),
    ]
    scores = [
        jnp.where(seen, block_scores(query_norm, keys, scale), -jnp.inf) for keys, _, seen in blocks
    ]
    top = reduce(jnp.maximum, [jnp.max(score, axis=2) for score in scores])
    total = reduce(jnp.add, [jnp.sum(jnp.exp(score - top[:, :, None]), axis=2) for score in scores])
    log_total = top + jnp.log(total)
    attended = reduce(
        jnp.add,
        [
            jnp.einsum(
                "hqk,khd->qhd",
                jnp.exp(score - log_total[:, :, None]).astype(jnp.bfloat16),
                block[1],
                preferred_element_type=jnp.float32,
            )
            for score, block in zip(scores, blocks)
        ],
    ).astype(jnp.bfloat16)
    delta = jnp.sum(grad_rows.astype(jnp.float32) * attended.astype(jnp.float32), axis=2).T
    query_delta = jnp.zeros((rows, heads, HDIM), jnp.float32)
    parts = []
    for (keys, block_values, seen), score in zip(blocks, scores):
        prob = jnp.exp(score - log_total[:, :, None])
        weight = prob.astype(jnp.bfloat16)
        dprob = jnp.einsum(
            "qhd,khd->hqk", grad_rows, block_values, preferred_element_type=jnp.float32
        )
        dscore = (prob * (dprob - delta[:, :, None])).astype(jnp.bfloat16)
        query_delta = (
            query_delta
            + jnp.einsum("hqk,khd->qhd", dscore, keys, preferred_element_type=jnp.float32) * scale
        )
        parts.append(key_terms(dscore, weight, query_norm, grad_rows, scale))
    key_acc, value_acc = parts[0]
    for offset in range(1, WINDOW + 1):
        if offset == 1:
            key_part, value_part = parts[1]
        else:
            mine = far_id == position - offset
            key_part = jnp.where(mine, parts[2][0], 0.0)
            value_part = jnp.where(mine, parts[2][1], 0.0)
        back_keys, back_values = shifted_2((key_part, value_part), "stretch", -offset)
        key_acc = key_acc + back_keys
        value_acc = value_acc + back_values
    slot_keys = jnp.stack(
        [jnp.where(sink_id == source, parts[3][0], 0.0) for source in range(SINK_POOL)]
    )
    slot_values = jnp.stack(
        [jnp.where(sink_id == source, parts[3][1], 0.0) for source in range(SINK_POOL)]
    )
    sink_keys_sum, sink_values_sum = lax.psum((slot_keys, slot_values), "stretch")
    for source in range(SINK_POOL):
        mine = position == source
        key_acc = key_acc + jnp.where(mine, sink_keys_sum[source], 0.0)
        value_acc = value_acc + jnp.where(mine, sink_values_sum[source], 0.0)
    query_scaled = query_gain * query_delta.reshape(rows, width)
    key_scaled = key_gain * key_acc.reshape(rows, width)
    query_inner, key_inner = lax.psum(
        (jnp.sum(query_scaled * query_float, axis=1), jnp.sum(key_scaled * key_float, axis=1)),
        "head",
    )
    query_grad = (
        query_inv * query_scaled - query_float * query_inv**3 * query_inner[:, None] / D
    ).astype(jnp.bfloat16)
    key_grad = (key_inv * key_scaled - key_float * key_inv**3 * key_inner[:, None] / D).astype(
        jnp.bfloat16
    )
    value_grad = value_acc.reshape(rows, width).astype(jnp.bfloat16)
    return (attended.reshape(rows, width), query_grad, key_grad, value_grad)


def solution(mesh):
    return jax.shard_map(
        per_device,
        mesh=mesh,
        in_specs=(
            P("stretch", "head"),
            P("stretch", "head"),
            P("stretch", "head"),
            P("head"),
            P("head"),
            P("stretch", None),
            P("stretch", None),
            P("stretch", "head"),
        ),
        out_specs=(
            P("stretch", "head"),
            P("stretch", "head"),
            P("stretch", "head"),
            P("stretch", "head"),
        ),
        check_vma=False,
    )
```

profile of v0, /device:TPU:1, one launch (start us, length us, event | category | flops | bytes accessed | tf_op | source)
XLA Modules:
  0.0 566.2 jit_solution(1828399054919212156)
XLA Ops:
  9.9 21.4 %all-reduce.2 = (f32[256]{0:T(256)S(1)}, f32[256]{0:T(256)S(1)}) all-reduce(f32[256]{0:T(256)S(1)} %get-tuple-element.52, f32[256]{0:T(256)S(1)} %get-tuple-element.53), channel_id=1, replica_groups=mesh['stretch'=32,'head'=8] {'head'}, use_global_device_ids=true, to_apply=%region_1.0 | all-reduce | flops 512 | bytes 4096 | tf_op jit(solution)/shard_map/psum | solution.py:47
  33.1 1.8 broadcast_select_fusion
  34.9 1.9 broadcast_select_fusion.1
  36.9 10.0 %collective-permute-start.5 = (bf16[256,5,128]{0,2,1:T(8,128)(2,1)}, bf16[256,5,128]{0,2,1:T(8,128)(2,1)}, u32[]{:S(2)}, u32[]{:S(2)}) collective-permute-start(bf16[256,5,128]{0,2,1:T(8,128)(2,1)} %bitcast.5), channel_id=1, source_target_pairs={{0,24},{8,32},{16,40},{24,48},{32,56},{40,64},{48,72},{56,80},{64,... | collective-permute-start | bytes 983048 | tf_op jit(solution)/shard_map/ppermute | solution.py:20
  46.8 3.5 collective-permute-start.4
  50.4 2.2 collective-permute-start.2
  52.6 4.8 collective-permute-start.1
  58.5 2.9 collective-permute-start
  61.7 1.4 fusion.70
  66.4 18.1 %collective-permute-done = bf16[256,5,128]{2,0,1:T(8,128)(2,1)S(1)} collective-permute-done((bf16[256,5,128]{2,0,1:T(8,128)(2,1)S(1)}, bf16[256,5,128]{2,0,1:T(8,128)(2,1)S(1)}, u32[]{:S(2)}, u32[]{:S(2)}) %collective-permute-start) | collective-permute-done | bytes 327712 | tf_op jit(solution)/shard_map/ppermute | solution.py:20
  85.3 4.4 collective-permute-start.3
  91.0 2.5 fusion.69
  93.5 172.8 %all-reduce.9.cloned.1.call-done = (bf16[256,5,128]{0,2,1:T(8,128)(2,1)}, bf16[256,5,128]{0,2,1:T(8,128)(2,1)}, bf16[256,5,128]{0,2,1:T(8,128)(2,1)}, bf16[256,5,128]{0,2,1:T(8,128)(2,1)}) async-done(((bf16[256,5,128]{0,2,1:T(8,128)(2,1)}, bf16[256,5,128]{0,2,1:T(8,128)(2,1)}, bf16[256,5,128]{0,2,1:T(8,128)(2,1)}, bf16[256,5,128]{0,2,1:T(8,128)(2,1)}), (bf16[256,5,128]{0,2,1:T(8,128)(2,1)}, ...) | async-done | bytes 1310736 | tf_op jit(solution)/shard_map/psum | solution.py:25
  266.3 1.5 fusion.68
  271.0 1.3 convolution_bitcast_fusion.3
  272.4 2.1 multiply_reduce_fusion
  275.7 1.9 copy.104
  277.6 1.8 select_bitcast_fusion.1
  280.7 1.4 fusion.10
  282.1 1.4 select_bitcast_fusion.7
  288.6 1.4 fusion.11
  290.3 2.4 collective-permute-start.6
  292.8 1.6 select_bitcast_fusion.3
  296.9 1.4 fusion.12
  298.3 1.5 fusion.76
  305.5 1.9 collective-permute-start.9
  307.5 17.6 %collective-permute-done.8 = f32[256,5,128]{0,2,1:T(8,128)} collective-permute-done((f32[256,5,128]{0,2,1:T(8,128)}, f32[256,5,128]{0,2,1:T(8,128)}, u32[]{:S(2)}, u32[]{:S(2)}) %collective-permute-start.8) | collective-permute-done | bytes 655392 | tf_op jit(solution)/shard_map/ppermute | solution.py:20
  325.0 2.6 collective-permute-done.6
  327.7 202.4 %all-reduce.7.cloned.1.call-done = (f32[2,256,5,128]{1,3,2,0:T(8,128)}, f32[2,256,5,128]{1,3,2,0:T(8,128)}) async-done(((f32[2,256,5,128]{1,3,2,0:T(8,128)}, f32[2,256,5,128]{1,3,2,0:T(8,128)}), (f32[2,256,5,128]{1,3,2,0:T(8,128)}, f32[2,256,5,128]{1,3,2,0:T(8,128)})) %all-reduce.7.cloned.1.call-update) | async-done | bytes 2621456 | tf_op jit(solution)/shard_map/psum | solution.py:137
  530.1 2.5 fusion.23
  532.8 20.0 %all-reduce.1 = (f32[256]{0:T(256)S(1)}, f32[256]{0:T(256)S(1)}) all-reduce(f32[256]{0:T(256)S(1)} %fusion.43, f32[256]{0:T(256)S(1)} %fusion.51), channel_id=1, replica_groups=mesh['stretch'=32,'head'=8] {'head'}, use_global_device_ids=true, to_apply=%region_18.19 | all-reduce | flops 512 | bytes 4096 | tf_op jit(solution)/shard_map/psum | solution.py:144
  556.2 2.3 fusion.31
  (102 shorter events, 32.4 us)
Async XLA Ops:
  7.2 24.1 %copy-start.21 = (bf16[256,640]{1,0:T(8,128)(2,1)S(1)}, bf16[256,640]{1,0:T(8,128)(2,1)}, u32[]{:S(2)}) copy-start(bf16[256,640]{1,0:T(8,128)(2,1)} %param.10) | copy-start | bytes 983044
  7.2 259.1 %all-reduce.9.cloned.1.call-start = ((), (), s32[]{:S(2)}) async-start(), calls=%async_computation.1 | async-start | bytes 2621440 | tf_op jit(solution)/shard_map/psum | solution.py:25
  7.2 25.0 %copy-start.24 = (f32[640]{0:T(1024)S(1)}, f32[640]{0:T(1024)}, u32[]{:S(2)}) copy-start(f32[640]{0:T(1024)} %param.12) | copy-start | bytes 7684
  8.4 53.1 %copy-start.6 = (bf16[256,640]{0,1:T(8,128)(2,1)}, bf16[256,640]{0,1:T(8,128)(2,1)S(1)}, u32[]{:S(2)}) copy-start(bf16[256,640]{0,1:T(8,128)(2,1)S(1)} %copy.60) | copy-start | bytes 983044
  9.7 25.2 %copy-start.4 = (bf16[256,640]{0,1:T(8,128)(2,1)}, bf16[256,640]{0,1:T(8,128)(2,1)S(1)}, u32[]{:S(2)}) copy-start(bf16[256,640]{0,1:T(8,128)(2,1)S(1)} %copy.61) | copy-start | bytes 983044
  34.9 26.6 %copy-start.23 = (f32[640]{0:T(1024)S(1)}, f32[640]{0:T(1024)}, u32[]{:S(2)}) copy-start(f32[640]{0:T(1024)} %param.11) | copy-start | bytes 7684
  36.8 493.3 %all-reduce.7.cloned.1.call-start = ((), (), s32[]{:S(2)}) async-start(), calls=%async_computation | async-start | bytes 5242880 | tf_op jit(solution)/shard_map/psum | solution.py:137
  36.9 234.1 %collective-permute-start.5 = (bf16[256,5,128]{0,2,1:T(8,128)(2,1)}, bf16[256,5,128]{0,2,1:T(8,128)(2,1)}, u32[]{:S(2)}, u32[]{:S(2)}) collective-permute-start(bf16[256,5,128]{0,2,1:T(8,128)(2,1)} %bitcast.5), channel_id=1, source_target_pairs={{0,24},{8,32},{16,40},{24,48},{32,56},{40,64},{48,72},{56,80},{64,... | collective-permute-start | bytes 983048 | tf_op jit(solution)/shard_map/ppermute | solution.py:20
  46.8 224.2 %collective-permute-start.4 = (bf16[256,5,128]{0,2,1:T(8,128)(2,1)}, bf16[256,5,128]{0,2,1:T(8,128)(2,1)}, u32[]{:S(2)}, u32[]{:S(2)}) collective-permute-start(bf16[256,5,128]{0,2,1:T(8,128)(2,1)} %bitcast.5), channel_id=1, source_target_pairs={{0,16},{8,24},{16,32},{24,40},{32,48},{40,56},{48,64},{56,72},{64,... | collective-permute-start | bytes 983048 | tf_op jit(solution)/shard_map/ppermute | solution.py:20
  50.4 40.6 %collective-permute-start.2 = (bf16[256,5,128]{0,2,1:T(8,128)(2,1)}, bf16[256,5,128]{0,2,1:T(8,128)(2,1)}, u32[]{:S(2)}, u32[]{:S(2)}) collective-permute-start(bf16[256,5,128]{0,2,1:T(8,128)(2,1)} %bitcast.1), channel_id=1, source_target_pairs={{0,24},{8,32},{16,40},{24,48},{32,56},{40,64},{48,72},{56,80},{64,... | collective-permute-start | bytes 983048 | tf_op jit(solution)/shard_map/ppermute | solution.py:20
  52.6 38.4 %collective-permute-start.1 = (bf16[256,5,128]{0,2,1:T(8,128)(2,1)}, bf16[256,5,128]{0,2,1:T(8,128)(2,1)}, u32[]{:S(2)}, u32[]{:S(2)}) collective-permute-start(bf16[256,5,128]{0,2,1:T(8,128)(2,1)} %bitcast.1), channel_id=1, source_target_pairs={{0,16},{8,24},{16,32},{24,40},{32,48},{40,56},{48,64},{56,72},{64,... | collective-permute-start | bytes 983048 | tf_op jit(solution)/shard_map/ppermute | solution.py:20
  58.5 26.0 %collective-permute-start = (bf16[256,5,128]{2,0,1:T(8,128)(2,1)S(1)}, bf16[256,5,128]{2,0,1:T(8,128)(2,1)S(1)}, u32[]{:S(2)}, u32[]{:S(2)}) collective-permute-start(bf16[256,5,128]{2,0,1:T(8,128)(2,1)S(1)} %copy.64), channel_id=1, source_target_pairs={{0,8},{8,16},{16,24},{24,32},{32,40},{40,48},{48,56},{56,64},{64,7... | collective-permute-start | bytes 983048 | tf_op jit(solution)/shard_map/ppermute | solution.py:20
  61.5 2.2 copy-start.25
  61.5 4.7 copy-start.22
  85.3 187.1 %collective-permute-start.3 = (bf16[256,5,128]{0,2,1:T(8,128)(2,1)}, bf16[256,5,128]{0,2,1:T(8,128)(2,1)}, u32[]{:S(2)}, u32[]{:S(2)}) collective-permute-start(bf16[256,5,128]{0,2,1:T(8,128)(2,1)} %bitcast.5), channel_id=1, source_target_pairs={{0,8},{8,16},{16,24},{24,32},{32,40},{40,48},{48,56},{56,64},{64,7... | collective-permute-start | bytes 983048 | tf_op jit(solution)/shard_map/ppermute | solution.py:20
  267.8 6.7 %copy-start.3 = (f32[5,256,256]{1,2,0:T(8,128)}, f32[5,256,256]{1,2,0:T(8,128)S(1)}, u32[]{:S(2)}) copy-start(f32[5,256,256]{1,2,0:T(8,128)S(1)} %get-tuple-element.43) | copy-start | bytes 3932164
  267.8 1.5 copy-start.18
  277.6 1.8 copy-start.11
  282.1 5.2 copy-start.13
  283.5 22.0 %collective-permute-start.7 = (f32[256,5,128]{0,2,1:T(8,128)}, f32[256,5,128]{0,2,1:T(8,128)}, u32[]{:S(2)}, u32[]{:S(2)}) collective-permute-start(f32[256,5,128]{0,2,1:T(8,128)} %get-tuple-element.32), channel_id=1, source_target_pairs={{16,0},{24,8},{32,16},{40,24},{48,32},{56,40},{64,48},{72,56},{80,... | collective-permute-start | bytes 1966088 | tf_op jit(solution)/shard_map/ppermute | solution.py:20
  284.8 40.2 %collective-permute-start.8 = (f32[256,5,128]{0,2,1:T(8,128)}, f32[256,5,128]{0,2,1:T(8,128)}, u32[]{:S(2)}, u32[]{:S(2)}) collective-permute-start(f32[256,5,128]{0,2,1:T(8,128)} %get-tuple-element.33), channel_id=1, source_target_pairs={{24,0},{32,8},{40,16},{48,24},{56,32},{64,40},{72,48},{80,56},{88,... | collective-permute-start | bytes 1966088 | tf_op jit(solution)/shard_map/ppermute | solution.py:20
  290.0 2.8 copy-start.2
  290.3 37.3 %collective-permute-start.6 = (f32[256,5,128]{0,2,1:T(8,128)S(1)}, f32[256,5,128]{0,2,1:T(8,128)}, u32[]{:S(2)}, u32[]{:S(2)}) collective-permute-start(f32[256,5,128]{0,2,1:T(8,128)S(1)} %fusion.15), channel_id=1, source_target_pairs={{8,0},{16,8},{24,16},{32,24},{40,32},{48,40},{56,48},{64,56},{72,6... | collective-permute-start | bytes 1966088 | tf_op jit(solution)/shard_map/ppermute | solution.py:20
  294.3 261.8 %collective-permute-start.10 = (f32[256,5,128]{0,2,1:T(8,128)}, f32[256,5,128]{0,2,1:T(8,128)}, u32[]{:S(2)}, u32[]{:S(2)}) collective-permute-start(f32[256,5,128]{0,2,1:T(8,128)} %get-tuple-element.26), channel_id=1, source_target_pairs={{16,0},{24,8},{32,16},{40,24},{48,32},{56,40},{64,48},{72,56},{80,... | collective-permute-start | bytes 1966088 | tf_op jit(solution)/shard_map/ppermute | solution.py:20
  295.6 260.5 %collective-permute-start.11 = (f32[256,5,128]{0,2,1:T(8,128)}, f32[256,5,128]{0,2,1:T(8,128)}, u32[]{:S(2)}, u32[]{:S(2)}) collective-permute-start(f32[256,5,128]{0,2,1:T(8,128)} %get-tuple-element.27), channel_id=1, source_target_pairs={{24,0},{32,8},{40,16},{48,24},{56,32},{64,40},{72,48},{80,56},{88,... | collective-permute-start | bytes 1966088 | tf_op jit(solution)/shard_map/ppermute | solution.py:20
  298.3 1.9 copy-start.9
  298.3 1.5 copy-start.12
  298.3 1.6 copy-start.20
  302.0 2.2 copy-start.7
  305.5 250.6 %collective-permute-start.9 = (f32[256,5,128]{0,2,1:T(8,128)}, f32[256,5,128]{0,2,1:T(8,128)}, u32[]{:S(2)}, u32[]{:S(2)}) collective-permute-start(f32[256,5,128]{0,2,1:T(8,128)} %convolution_bitcast_fusion), channel_id=1, source_target_pairs={{8,0},{16,8},{24,16},{32,24},{40,32},{48,40},{56,48},{64,56},{72,6... | collective-permute-start | bytes 1966088 | tf_op jit(solution)/shard_map/ppermute | solution.py:20
  530.1 2.6 copy-start.5
  530.1 22.8 %copy-start.8 = (bf16[256,640]{0,1:T(8,128)(2,1)S(1)}, bf16[256,640]{0,1:T(8,128)(2,1)}, u32[]{:S(2)}) copy-start(bf16[256,640]{0,1:T(8,128)(2,1)} %copy-done.6) | copy-start | bytes 983044
  (8 other events, 9.2 us)
Sparse Core Ops, SparseCore 0:
  36.9 229.2 all-reduce.8
  288.7 241.3 all-reduce.6
where the time goes:
time: 569 us; the launch traced here: 566 us
  waiting for transfers between devices  414 us (73%)
  blocking collectives  41.5 us (7%)
  starting transfers between devices  37.4 us (7%)
  matrix products  32.1 us (6%)
  between operations  17.1 us (3%)
  local copies, waits for them, and re-layouts  14.8 us (3%)
  other arithmetic  9.86 us (2%)
    psum x1, waiting for transfers between devices, per_device(): lax.psum((slot_keys, slot_values), 'stretch')  202 us
    psum x1, waiting for transfers between devices, broadcast(): return lax.psum(kept, axis)  173 us
    ppermute x12, waiting for transfers between devices, shifted_2(): return lax.ppermute(x, axis, pairs)  38.3 us
    ppermute x12, starting transfers between devices, shifted_2(): return lax.ppermute(x, axis, pairs)  37.3 us
    psum x1, blocking collectives, per_device(): lax.psum((jnp.sum(query_float * query_float, axis=1), jnp.sum(key_float *...  21.4 us
    psum x1, blocking collectives, per_device(): lax.psum((jnp.sum(query_scaled * query_float, axis=1), jnp.sum(key_scaled...  20 us
    unnamed x60, local copies, waits for them, and re-layouts  13 us
  transfers between devices with their start and end apart: 14, of which 5 were waited for; matrix products, arithmetic and copies ran while one was open for 5% of the time, Pallas kernels for 0%

commit v1 on v0

v1 whole, which is shorter than its diff:
```python
import jax
import jax.numpy as jnp
from jax import lax
from jax.experimental import pallas as pl
from jax.experimental.pallas import tpu as pltpu
from jax.sharding import PartitionSpec as P

D = 5120
HDIM = 128
TOKC = 256
HEADS = 5
STRETCHES = 32
HEAD_DEVICES = 8
EPS = 1e-06
SCALE = HDIM ** (-0.5)
SCALE2 = SCALE * 1.4426950408889634
FAR_AWAY = 1e30
MESH = pl.DeviceIdType.MESH
F32 = jnp.float32
BF16 = jnp.bfloat16


def dot_t(a, b):
    return lax.dot_general(a, b, (((1,), (1,)), ((), ())), preferred_element_type=F32)


def dot_n(a, b):
    return lax.dot_general(a, b, (((1,), (0,)), ((), ())), preferred_element_type=F32)


def to_rows(columns):
    lane = lax.broadcasted_iota(jnp.int32, (TOKC, HDIM), 1)
    spread = jnp.zeros((TOKC, HDIM), F32)
    for i, column in enumerate(columns):
        spread = jnp.where(lane == i, column, spread)
    return spread.T[:8]


def to_full(row):
    return jnp.broadcast_to(row, (HDIM, TOKC)).T


def remote(src, dst, send, recv, device):
    return pltpu.make_async_remote_copy(
        src_ref=src, dst_ref=dst, send_sem=send, recv_sem=recv, device_id=device, device_id_type=MESH
    )


def kernel(
    query_hbm, key_hbm, values_hbm, grad_hbm, query_gain, key_gain, recent, sink,
    att_out, dq_out, dk_out, dv_out,
    raw, kv, qd, kvr, qdr, sinkb, red, rr1, rr2, acc, up, dq, dk, dv, stat, statr, tile, tiler, inv,
    load_sem, kvs, kvrs, qds, qdrs, sks, skc, skr, sts, strs, ars, arr, rs1, rr1s, rs2, rr2s,
):
    c = lax.axis_index("stretch")
    g = lax.axis_index("head")
    par = c % 2
    z = (c // 2) % 8
    y = c // 16
    j = y * 2 + par

    def dev(stretch):
        return (stretch % STRETCHES, g)

    partner = (c + 1 - 2 * par, g)
    is_root = c < 2
    nonroot_rep = jnp.logical_and(z >= 1, y == par)
    is_rep = jnp.logical_or(is_root, nonroot_rep)
    parent_z = jnp.where((z == 3) | (z == 4), 2, jnp.where((z == 5) | (z == 6), 7, 0))
    parent = (jnp.where(parent_z == 0, par, 2 * parent_z + 17 * par), g)
    parent_slot = jnp.where((z == 2) | (z == 4) | (z == 5), 1, jnp.where(z == 7, 2, 0))
    rep_j = jnp.where(z == 0, par, 3 * par)

    def member(i):
        at = (rep_j + 1 + i) % 4
        return ((at // 2) * 16 + 2 * z + at % 2, g)

    def child(child_z):
        return (2 * child_z + 17 * par, g)

    children = ((0, (1, 2, 7)), (2, (3, 4)), (7, (6, 5)))

    order = ((0, 0, key_hbm, raw, 1), (1, 1, query_hbm, raw, 0), (2, 2, values_hbm, kv, 0), (3, 3, grad_hbm, qd, 0))

    def load(i, hbm, dst, part, h):
        return pltpu.make_async_copy(
            hbm.at[:, pl.ds(h * HDIM, HDIM)], dst.at[part, h], load_sem.at[i, h]
        )

    for i, _, hbm, dst, part in order:
        for h in range(HEADS):
            load(i, hbm, dst, part, h).start()

    barrier = pltpu.get_barrier_semaphore()

    def greet(device):
        pl.semaphore_signal(barrier, inc=1, device_id=device, device_id_type=MESH)

    for step in (1, 2, 3):
        greet(dev(c + step))
        greet(dev(c - step + STRETCHES))
    greet(dev(c + 16))
    greet(dev(c + 17 - 2 * par))
    for step in range(1, HEAD_DEVICES):
        greet((c, (g + step) % HEAD_DEVICES))

    @pl.when(jnp.logical_and(is_rep, jnp.logical_not(is_root)))
    def _():
        greet(parent)

    for at_z, kids in children:
        @pl.when(jnp.logical_and(is_rep, z == at_z))
        def _():
            for kid in kids:
                greet(child(kid))

    squares = []
    for i, part in ((1, 0), (0, 1)):
        total = jnp.zeros((TOKC, 1), F32)
        for h in range(HEADS):
            load(i, key_hbm, raw, part, h).wait()
            block = raw[part, h].astype(F32)
            total = total + jnp.sum(block * block, axis=1, keepdims=True)
        squares.append(total)
    tile[0] = to_rows(squares)

    edges = jnp.where(z == 0, 3, jnp.where((z == 2) | (z == 7), 2, 0)) + jnp.where(z == 0, 0, 1)
    pl.semaphore_wait(barrier, 15 + jnp.where(is_rep, edges, 0))

    def reduce_copy(phase, step):
        return remote(
            tile.at[phase], tiler.at[phase, step - 1], ars.at[phase, step - 1], arr.at[phase, step - 1],
            (c, (g + step) % HEAD_DEVICES),
        )

    def reduce_start(phase):
        for step in range(1, HEAD_DEVICES):
            reduce_copy(phase, step).start()

    def reduce_finish(phase):
        total = tile[phase]
        for step in range(1, HEAD_DEVICES):
            reduce_copy(phase, step).wait_recv()
            total = total + tiler[phase, step - 1]
        return total

    reduce_start(0)

    def kv_copies(p, h):
        return (
            remote(kv.at[p, h], kvr.at[1, p, h], kvs.at[0, p, h], kvrs.at[1, p, h], dev(c + 2)),
            remote(
                kv.at[p, h], kvr.at[2 * par, p, h], kvs.at[1, p, h], kvrs.at[2 * par, p, h],
                dev(c + 1 + 2 * par),
            ),
        )

    def qd_copies(p, h):
        return (
            remote(qd.at[p, h], qdr.at[1, p, h], qds.at[0, p, h], qdrs.at[1, p, h], dev(c + STRETCHES - 2)),
            remote(
                qd.at[p, h], qdr.at[2 - 2 * par, p, h], qds.at[1, p, h], qdrs.at[2 - 2 * par, p, h],
                dev(c + STRETCHES - 3 + 2 * par),
            ),
        )

    def kv_forward(p, h):
        return remote(
            kvr.at[1, p, h], kvr.at[2 - 2 * par, p, h], kvs.at[2, p, h], kvrs.at[2 - 2 * par, p, h], partner
        )

    def qd_forward(p, h):
        return remote(
            qdr.at[1, p, h], qdr.at[2 * par, p, h], qds.at[2, p, h], qdrs.at[2 * par, p, h], partner
        )

    def kv_arrived(slot, p, h):
        remote(kvr.at[slot, p, h], kvr.at[slot, p, h], kvs.at[0, p, h], kvrs.at[slot, p, h], partner).wait_recv()

    def qd_arrived(slot, p, h):
        remote(qdr.at[slot, p, h], qdr.at[slot, p, h], qds.at[0, p, h], qdrs.at[slot, p, h], partner).wait_recv()

    def sink_arrived(s, p, h):
        remote(sinkb.at[s, p, h], sinkb.at[s, p, h], sks.at[0, p, h], skr.at[s, p, h], partner).wait_recv()

    def member_copy(i, p, h):
        return remote(sinkb.at[par, p, h], sinkb.at[par, p, h], sks.at[i, p, h], skr.at[par, p, h], member(i))

    def child_copy(i, kid, p, h):
        return remote(sinkb.at[par, p, h], sinkb.at[par, p, h], skc.at[i, p, h], skr.at[par, p, h], child(kid))

    def sink_send(p, h):
        for at_z, kids in children:
            @pl.when(z == at_z)
            def _():
                for i, kid in enumerate(kids):
                    child_copy(i, kid, p, h).start()

        for i in range(3):
            member_copy(i, p, h).start()

    def send(p, h):
        @pl.when(is_root)
        def _():
            sinkb[par, p, h] = kv[p, h]
            sink_send(p, h)

        for copy in kv_copies(p, h) + qd_copies(p, h):
            copy.start()

    def forward(p, h):
        @pl.when(nonroot_rep)
        def _():
            sink_arrived(par, p, h)
            sink_send(p, h)

        kv_arrived(1, p, h)
        kv_forward(p, h).start()
        qd_arrived(1, p, h)
        qd_forward(p, h).start()

    def loop(count, body):
        lax.fori_loop(0, count, lambda h, _: (body(h), 0)[1], 0)

    for h in range(HEADS):
        load(2, values_hbm, kv, 0, h).wait()
        load(3, grad_hbm, qd, 0, h).wait()
    loop(HEADS, lambda h: send(0, h))

    inverse = lax.rsqrt(reduce_finish(0) / D + EPS)
    inv[0] = to_full(inverse[0:1])
    inv[1] = to_full(inverse[1:2])

    def normalize(h):
        qd[1, h] = (raw[0, h].astype(F32) * inv[0] * query_gain[h]).astype(BF16)
        kv[1, h] = (raw[1, h].astype(F32) * inv[1] * key_gain[h]).astype(BF16)
        send(1, h)

    loop(HEADS, normalize)
    loop(HEADS, lambda h: forward(0, h))

    far = recent[0, 1]
    sink_id = sink[0, 0]
    far_two = jnp.logical_and(far == c - 2, c >= 2)
    far_three = jnp.logical_and(far == c - 3, c >= 3)
    two = jnp.where(far_two, 1.0, 0.0).astype(F32)
    sink_one = jnp.where(sink_id == 1, 1.0, 0.0).astype(F32)
    sink_zero = jnp.where(sink_id == 0, 1.0, 0.0).astype(F32)
    near_off = jnp.where(c >= 1, 0.0, FAR_AWAY).astype(F32)
    two_off = jnp.where(far_two, 0.0, FAR_AWAY).astype(F32)
    three_off = jnp.where(far_three, 0.0, FAR_AWAY).astype(F32)
    far_off = jnp.minimum(two_off, three_off)
    sink_off = jnp.where(sink_id >= 0, 0.0, FAR_AWAY).astype(F32)

    def mix(first, second, share):
        return (first.astype(F32) * share + second.astype(F32) * (1.0 - share)).astype(BF16)

    def key_side(keys, vals, queries, grads, log_row, delta_row):
        prob = jnp.exp2(dot_t(keys, queries) * SCALE2 - log_row)
        dprob = dot_t(vals, grads)
        dscore = (prob * (dprob - delta_row)).astype(BF16)
        return dot_n(dscore, queries), dot_n(prob.astype(BF16), grads)

    def stat_copy(step, h):
        return remote(
            stat.at[h], statr.at[step - 1, h], sts.at[step - 1, h], strs.at[step - 1, h], dev(c + STRETCHES - step)
        )

    def rep_of(s):
        return 2 * z if s == 0 else jnp.where(z == 0, 1, 2 * z + 17)

    def rep_at(s):
        return 0 if s == 0 else jnp.where(z == 0, 1, 3)

    def partial_copy(s, h):
        slot = (j - rep_at(s) + 3) % 4
        return remote(
            red.at[s, h], rr1.at[slot, h], rs1.at[s, h], rr1s.at[slot, h], (rep_of(s), g)
        )

    def query_side(h):
        for p in (0, 1):
            kv_arrived(0, p, h)
            kv_arrived(2, p, h)
            sink_arrived(1 - par, p, h)

            @pl.when(jnp.logical_not(is_rep))
            def _():
                sink_arrived(par, p, h)

        queries, grads = qd[1, h], qd[0, h]
        sink_keys = mix(sinkb[1, 1, h], sinkb[0, 1, h], sink_one)
        sink_vals = mix(sinkb[1, 0, h], sinkb[0, 0, h], sink_one)
        blocks = (
            (kv[1, h], kv[0, h], 0.0),
            (kvr[0, 1, h], kvr[0, 0, h], near_off),
            (mix(kvr[1, 1, h], kvr[2, 1, h], two), mix(kvr[1, 0, h], kvr[2, 0, h], two), far_off),
            (sink_keys, sink_vals, sink_off),
        )
        scores = [dot_t(queries, keys) * SCALE2 for keys, _, _ in blocks]
        top = None
        for score, block in zip(scores, blocks):
            here = jnp.max(score, axis=1, keepdims=True) - block[2]
            top = here if top is None else jnp.maximum(top, here)
        probs = [jnp.exp2(score - (top + block[2])) for score, block in zip(scores, blocks)]
        total = None
        for prob in probs:
            here = jnp.sum(prob, axis=1, keepdims=True)
            total = here if total is None else total + here
        share = 1.0 / total
        attended = jnp.zeros((TOKC, HDIM), F32)
        probs = [prob * share for prob in probs]
        for prob, block in zip(probs, blocks):
            attended = attended + dot_n(prob.astype(BF16), block[1])
        attended = attended.astype(BF16)
        att_out[:, pl.ds(pl.multiple_of(h * HDIM, HDIM), HDIM)] = attended
        delta = jnp.sum(grads.astype(F32) * attended.astype(F32), axis=1, keepdims=True)
        log_total = top + jnp.log2(total)
        rows = to_rows(
            (
                log_total, delta, log_total + near_off, log_total + two_off, log_total + three_off,
                log_total + sink_off,
            )
        )
        stat[h] = rows
        for step in (1, 2, 3):
            stat_copy(step, h).start()
        sink_dk, sink_dv = key_side(sink_keys, sink_vals, queries, grads, rows[5:6], rows[1:2])
        for s, mine in ((0, sink_zero), (1, sink_one)):
            red[s, h, 0] = (sink_dk * mine).astype(BF16)
            red[s, h, 1] = (sink_dv * mine).astype(BF16)

            @pl.when(c != rep_of(s))
            def _():
                partial_copy(s, h).start()

        query_delta = jnp.zeros((TOKC, HDIM), F32)
        for prob, block in zip(probs, blocks):
            dscore = (prob * (dot_t(grads, block[1]) - delta)).astype(BF16)
            query_delta = query_delta + dot_n(dscore, block[0])
        dq[h] = query_delta * SCALE

    def owner_side(h):
        keys, vals = kv[1, h], kv[0, h]
        key_sum, value_sum = key_side(keys, vals, qd[1, h], qd[0, h], stat[h, 0:1], stat[h, 1:2])
        for slot in range(3):
            for p in (0, 1):
                if slot != 1:
                    qd_arrived(slot, p, h)
            stat_copy(slot + 1, h).wait_recv()
            more_keys, more_values = key_side(
                keys, vals, qdr[slot, 1, h], qdr[slot, 0, h],
                statr[slot, h, slot + 2:slot + 3], statr[slot, h, 1:2],
            )
            key_sum, value_sum = key_sum + more_keys, value_sum + more_values
        dk[h] = key_sum
        dv[h] = value_sum

    def up_copy(h):
        return remote(up.at[h], rr2.at[parent_slot, h], rs2.at[h], rr2s.at[parent_slot, h], parent)

    def plane_sum(h):
        for slot in range(3):
            remote(rr1.at[slot, h], rr1.at[slot, h], rs1.at[0, h], rr1s.at[slot, h], partner).wait_recv()
        for part in (0, 1):
            total = red[par, h, part].astype(F32)
            for slot in range(3):
                total = total + rr1[slot, h, part].astype(F32)
            acc[h, part] = total

        @pl.when(jnp.logical_and(z % 7 != 0, z != 2))
        def _():
            up[h] = acc[h].astype(BF16)
            up_copy(h).start()

    def children_sum(h, count):
        for slot in range(count):
            remote(rr2.at[slot, h], rr2.at[slot, h], rs2.at[h], rr2s.at[slot, h], partner).wait_recv()
        for part in (0, 1):
            total = acc[h, part]
            for slot in range(count):
                total = total + rr2[slot, h, part].astype(F32)
            acc[h, part] = total

    def step(at):
        @pl.when(at < HEADS)
        def _():
            forward(1, at)

        @pl.when(jnp.logical_and(at >= 1, at <= HEADS))
        def _():
            query_side(at - 1)

        @pl.when(jnp.logical_and(at >= 2, at <= HEADS + 1))
        def _():
            owner_side(at - 2)

            @pl.when(is_rep)
            def _():
                plane_sum(at - 2)

        @pl.when(jnp.logical_and(at >= 3, at <= HEADS + 2))
        def _():
            @pl.when(jnp.logical_and(nonroot_rep, jnp.logical_or(z == 2, z == 7)))
            def _():
                children_sum(at - 3, 2)
                up[at - 3] = acc[at - 3].astype(BF16)
                up_copy(at - 3).start()

        @pl.when(jnp.logical_and(at >= 4, at <= HEADS + 3))
        def _():
            @pl.when(is_root)
            def _():
                children_sum(at - 4, 3)
                dk[at - 4] = dk[at - 4] + acc[at - 4, 0]
                dv[at - 4] = dv[at - 4] + acc[at - 4, 1]

    loop(HEADS + 4, step)

    def inner(h, sums):
        query_sum, key_sum = sums
        query_sum = query_sum + jnp.sum(
            dq[h] * query_gain[h] * raw[0, h].astype(F32), axis=1, keepdims=True
        )
        key_sum = key_sum + jnp.sum(
            dk[h] * SCALE * key_gain[h] * raw[1, h].astype(F32), axis=1, keepdims=True
        )
        return query_sum, key_sum

    zero = jnp.zeros((TOKC, 1), F32)
    tile[1] = to_rows(lax.fori_loop(0, HEADS, inner, (zero, zero)))
    reduce_start(1)
    total = reduce_finish(1)
    query_inner = to_full(total[0:1]) * inv[0] * inv[0] * inv[0] / D
    key_inner = to_full(total[1:2]) * inv[1] * inv[1] * inv[1] / D
    tiler[1, 0] = total
    for h in range(HEADS):
        at = pl.ds(h * HDIM, HDIM)
        dq_out[:, at] = (
            dq[h] * query_gain[h] * inv[0] - raw[0, h].astype(F32) * query_inner
        ).astype(BF16)
        dk_out[:, at] = (
            dk[h] * SCALE * key_gain[h] * inv[1] - raw[1, h].astype(F32) * key_inner
        ).astype(BF16)
        dv_out[:, at] = dv[h].astype(BF16)

    def drain(h):
        for p in (0, 1):
            for copy in kv_copies(p, h) + qd_copies(p, h):
                copy.wait_send()
            kv_forward(p, h).wait_send()
            qd_forward(p, h).wait_send()

            @pl.when(is_rep)
            def _():
                for at_z, kids in children:
                    @pl.when(z == at_z)
                    def _():
                        for i, kid in enumerate(kids):
                            child_copy(i, kid, p, h).wait_send()

                for i in range(3):
                    member_copy(i, p, h).wait_send()

        for step in (1, 2, 3):
            stat_copy(step, h).wait_send()
        for s in (0, 1):
            @pl.when(c != rep_of(s))
            def _():
                partial_copy(s, h).wait_send()

        @pl.when(nonroot_rep)
        def _():
            up_copy(h).wait_send()

    loop(HEADS, drain)
    for phase in (0, 1):
        for step in range(1, HEAD_DEVICES):
            reduce_copy(phase, step).wait_send()


def per_device(query_raw, key_raw, values, query_gain, key_gain, recent_ids, sink_ids, out_grad):
    rows, width = query_raw.shape
    block = (HEADS, TOKC, HDIM)
    dma = pltpu.SemaphoreType.DMA
    any_spec = pl.BlockSpec(memory_space=pl.ANY)
    vmem = pl.BlockSpec(memory_space=pltpu.VMEM)
    smem = pl.BlockSpec(memory_space=pltpu.SMEM)
    return pl.pallas_call(
        kernel,
        out_shape=[jax.ShapeDtypeStruct((rows, width), BF16)] * 4,
        in_specs=[any_spec] * 4 + [vmem] * 2 + [smem] * 2,
        out_specs=[vmem] * 4,
        scratch_shapes=[
            pltpu.VMEM((2,) + block, BF16),
            pltpu.VMEM((2,) + block, BF16),
            pltpu.VMEM((2,) + block, BF16),
            pltpu.VMEM((3, 2) + block, BF16),
            pltpu.VMEM((3, 2) + block, BF16),
            pltpu.VMEM((2, 2) + block, BF16),
            pltpu.VMEM((2, HEADS, 2, TOKC, HDIM), BF16),
            pltpu.VMEM((3, HEADS, 2, TOKC, HDIM), BF16),
            pltpu.VMEM((3, HEADS, 2, TOKC, HDIM), BF16),
            pltpu.VMEM((HEADS, 2, TOKC, HDIM), F32),
            pltpu.VMEM((HEADS, 2, TOKC, HDIM), BF16),
            pltpu.VMEM(block, F32),
            pltpu.VMEM(block, F32),
            pltpu.VMEM(block, F32),
            pltpu.VMEM((HEADS, 8, TOKC), F32),
            pltpu.VMEM((3, HEADS, 8, TOKC), F32),
            pltpu.VMEM((2, 8, TOKC), F32),
            pltpu.VMEM((2, HEAD_DEVICES - 1, 8, TOKC), F32),
            pltpu.VMEM((2, TOKC, HDIM), F32),
            dma((4, HEADS)),
            dma((3, 2, HEADS)),
            dma((3, 2, HEADS)),
            dma((3, 2, HEADS)),
            dma((3, 2, HEADS)),
            dma((3, 2, HEADS)),
            dma((3, 2, HEADS)),
            dma((2, 2, HEADS)),
            dma((3, HEADS)),
            dma((3, HEADS)),
            dma((2, HEAD_DEVICES - 1)),
            dma((2, HEAD_DEVICES - 1)),
            dma((2, HEADS)),
            dma((3, HEADS)),
            dma((HEADS,)),
            dma((3, HEADS)),
        ],
        compiler_params=pltpu.CompilerParams(
            collective_id=0, has_side_effects=True, vmem_limit_bytes=48 * 2**20
        ),
        cost_estimate=pl.CostEstimate(flops=3 * 10**9, bytes_accessed=6 * 10**6, transcendentals=3 * 10**6),
        name="stretch_attention",
    )(
        query_raw, key_raw, values, out_grad,
        query_gain.reshape(HEADS, 1, HDIM), key_gain.reshape(HEADS, 1, HDIM),
        recent_ids, sink_ids,
    )


def solution(mesh):
    split = P("stretch", "head")
    return jax.shard_map(
        per_device,
        mesh=mesh,
        in_specs=(split, split, split, P("head"), P("head"), P("stretch", None), P("stretch", None), split),
        out_specs=(split,) * 4,
        check_vma=False,
    )
```

time: 569 us -> 122 us (0.21)
  waiting for transfers between devices: 414 us -> 0 us
  Pallas kernels: 0 us -> 112 us
  blocking collectives: 41.5 us -> 0 us
  starting transfers between devices: 37.4 us -> 0 us
  matrix products: 32.1 us -> 0 us
  between operations: 17.1 us -> 1.31 us
  other arithmetic: 9.86 us -> 0 us
  local copies, waits for them, and re-layouts: 14.8 us -> 8.14 us
    psum x2 -> x0, waiting for transfers between devices: 375 us -> none  [the longest x1 202 us: per_device(): lax.psum((slot_keys, slot_values), 'stretch')]
    pallas_call x0 -> x1, Pallas kernels: none -> 112 us  [per_device(): pl.pallas_call(kernel, out_shape=[jax.ShapeDtypeStruct((rows, width), BF1...]
    psum x2 -> x0, blocking collectives: 41.5 us -> none  [the longest x1 21.4 us: per_device(): lax.psum((jnp.sum(query_float * query_float, axis=1), jnp.sum(key_float *...]
    ppermute x12 -> x0, waiting for transfers between devices: 38.3 us -> none  [shifted_2(): return lax.ppermute(x, axis, pairs)]
    ppermute x12 -> x0, starting transfers between devices: 37.3 us -> none  [shifted_2(): return lax.ppermute(x, axis, pairs)]
    dot_general x24 -> x0, matrix products: 32.1 us -> none  [the longest x4 6.86 us: key_terms(): jnp.einsum('hqk,qhd->khd', weight, grads, preferred_element_type=jnp.floa...]
    unnamed x60 -> x16, local copies, waits for them, and re-layouts: 13 us -> 7.44 us
  transfers between devices with their start and end apart: 14 -> 0, of which waited for: 5 -> 0; matrix products, arithmetic and copies ran while one was open for 5% -> 0% of each run, Pallas kernels for 0% -> 0%
where the time goes in v1:
time: 122 us
  Pallas kernels  112 us (92%)
  local copies, waits for them, and re-layouts  8.14 us (7%)
  between operations  1.31 us (1%)
    pallas_call x1, Pallas kernels, per_device(): pl.pallas_call(kernel, out_shape=[jax.ShapeDtypeStruct((rows, width), BF1...  112 us
    unnamed x16, local copies, waits for them, and re-layouts  7.44 us

profile of v1, /device:TPU:1, one launch (start us, length us, event | category | flops | bytes accessed | tf_op | source)
XLA Modules:
  0.0 121.9 jit_solution(6797108231020402455)
XLA Ops:
  0.6 0.0 copy-start.5
  1.3 0.7 reshape.14.query_gain
  2.0 0.0 copy-done.5
  2.0 0.0 copy-start.4
  2.0 0.6 copy-done.4
  2.7 0.0 copy-start
  2.7 1.0 copy-done
  3.6 0.0 copy-start.1
  3.6 1.0 copy-done.1
  4.6 0.0 copy-start.2
  4.6 1.0 copy-done.2
  5.6 0.0 copy-start.3
  5.6 1.0 copy-done.3
  6.5 112.5 %stretch_attention.1 = (bf16[256,640]{1,0:T(8,128)(2,1)S(1)}, bf16[256,640]{1,0:T(8,128)(2,1)S(1)}, bf16[256,640]{1,0:T(8,128)(2,1)S(1)}, bf16[256,640]{1,0:T(8,128)(2,1)S(1)}) custom-call(bf16[256,640]{1,0:T(8,128)(2,1)S(1)} %copy-done, bf16[256,640]{1,0:T(8,128)(2,1)S(1)} %copy-done.1, bf16[256,640]{1,0:T(8,128)(2,1)S(1)} %copy-done.2, ...), custom_call_target="tpu_custom_call" | custom-call | flops 3000000000 | bytes 6000000 | tf_op jit(solution)/shard_map/stretch_attention/pallas_call | solution.py:489
  119.0 0.7 copy.17
  119.8 0.7 copy.18
  120.5 0.7 copy.19
  121.2 0.7 copy.20
  (1 shorter events, 0.0 us)
Async XLA Ops:
  0.6 1.4 %copy-start.5 = (f32[640]{0:T(1024)S(1)}, f32[640]{0:T(1024)}, u32[]{:S(2)}) copy-start(f32[640]{0:T(1024)} %param.12) | copy-start | bytes 7684
  2.0 0.7 copy-start.4
  2.7 1.0 copy-start
  3.6 1.0 copy-start.1
  4.6 1.0 copy-start.2
  5.6 1.0 copy-start.3

commit v2 on v1

v2 whole, which is shorter than its diff:
```python
import jax
import jax.numpy as jnp
from jax import lax
from jax.experimental import pallas as pl
from jax.experimental.pallas import tpu as pltpu
from jax.sharding import PartitionSpec as P

D = 5120
HDIM = 128
TOKC = 256
HEADS = 5
STRETCHES = 32
HEAD_DEVICES = 8
EPS = 1e-06
SCALE = HDIM ** (-0.5)
SCALE2 = SCALE * 1.4426950408889634
FAR_AWAY = 1e30
MESH = pl.DeviceIdType.MESH
NEAR = (1, 2, 3, -1, -2, -3)
KIDS = ({0: (1, 7), 1: (2,), 7: (6, 5), 5: (4, 3)}, {1: (2,), 7: (6, 5, 0), 5: (4, 3)})
VALUE_KIDS = (1, 7)
AHEAD = 2
SUMS = {0: (1, 7, 5), 1: (2,), 7: (6,), 5: (4, 3)}
F32 = jnp.float32
BF16 = jnp.bfloat16


def dot_t(a, b):
    return lax.dot_general(a, b, (((1,), (1,)), ((), ())), preferred_element_type=F32)


def dot_n(a, b):
    return lax.dot_general(a, b, (((1,), (0,)), ((), ())), preferred_element_type=F32)


def to_rows(columns):
    lane = lax.broadcasted_iota(jnp.int32, (TOKC, HDIM), 1)
    spread = jnp.zeros((TOKC, HDIM), F32)
    for i, column in enumerate(columns):
        spread = jnp.where(lane == i, column, spread)
    return spread.T[:8]


def to_full(row):
    return jnp.broadcast_to(row, (HDIM, TOKC)).T


def remote(src, dst, send, recv, device):
    return pltpu.make_async_remote_copy(
        src_ref=src, dst_ref=dst, send_sem=send, recv_sem=recv, device_id=device, device_id_type=MESH
    )


def kernel(
    query_hbm, key_hbm, values_hbm, grad_hbm, query_gain_hbm, key_gain_hbm, recent, sink,
    att_out, dq_out, dk_out, dv_out,
    kv, qd, keyn, queryn, kvr, qdr, sinkb, red, rr1, rr2, acc, up, vin, dq, dk, dv, stat, statr, tile, tiler, inv, gains, sinv, ninv, tsum, tout, tin,
    load_sem, gain_sem, kvs, kvrs, qds, qdrs, sks, skc, skr, sts, strs, ars, arr, rs1, rr1s, rs2, rr2s, vis, vir, crs, svs, svr, tis, tir, nis, nir,
):
    c = lax.axis_index("stretch")
    g = lax.axis_index("head")
    par = c % 2
    z = (c // 2) % 8
    y = c // 16
    part = 1 - y
    even = par == 0
    odd = par == 1
    owner = c < 2
    partner = (c + 1 - 2 * par, g)

    def dev(stretch):
        return (stretch % STRETCHES, g)

    def member(i):
        return (((y + i // 2) % 2) * 16 + 2 * z + (par + i % 2) % 2, g)

    def at_plane(other):
        return (y * 16 + 2 * other + par, g)

    loads = ((values_hbm, kv, 0), (key_hbm, kv, 1), (query_hbm, qd, 1), (grad_hbm, qd, 0))
    level = jnp.where((z == 1) | (z == 7), 1, jnp.where((z == 4) | (z == 3), 3, 2))
    level = jnp.where(owner, 0, level)
    lag_pass = jnp.where(owner, 0, 2 * level - 2)
    lag_relay = 2 * level
    lag_query = jnp.where(owner, 2, 2 * level + 1)
    paced = z == 1
    busy = (z == 7) | (z == 5)

    def load(i, h):
        hbm, dst, p = loads[i]
        return pltpu.make_async_copy(hbm.at[:, pl.ds(h * HDIM, HDIM)], dst.at[h, p], load_sem.at[i, h])

    def load_gain(i, hbm):
        return pltpu.make_async_copy(hbm, gains.at[i], gain_sem.at[i])

    for i in (1, 2, 0, 3):
        for h in range(HEADS):
            load(i, h).start()
    load_gain(0, query_gain_hbm).start()
    load_gain(1, key_gain_hbm).start()

    for missing, buffer, slot in (
        (c == 0, kvr, 0), (c < 2, kvr, 1), (c < 3, kvr, 2), (c > 30, qdr, 0), (c > 29, qdr, 1), (c > 28, qdr, 2),
    ):
        @pl.when(missing)
        def _():
            buffer[slot] = jnp.zeros((HEADS, 2, TOKC, HDIM), BF16)

    barrier = pltpu.get_barrier_semaphore()

    def greet(device):
        pl.semaphore_signal(barrier, inc=1, device_id=device, device_id_type=MESH)

    for shift in (1, 2, 3):
        greet(dev(c + shift))
        greet(dev(c - shift + STRETCHES))
    for i in (1, 2, 3):
        greet(member(i))
    for shift in range(1, HEAD_DEVICES):
        greet((c, (g + shift) % HEAD_DEVICES))

    def greet_all(i, _):
        @pl.when(i != c)
        def _():
            greet((i, g))

        return 0

    @pl.when(owner)
    def _():
        lax.fori_loop(0, STRETCHES, greet_all, 0)

    for root in (0, 1):
        @pl.when(c != root)
        def _():
            greet((root, g))

    degree = jnp.where(owner, STRETCHES, 2)
    for at_z in range(8):
        friends = sorted(set(KIDS[0].get(at_z, ()) + SUMS.get(at_z, ()) + tuple(
            top for table in (KIDS[0], SUMS) for top, below in table.items() if at_z in below)))
        degree = degree + jnp.where(z == at_z, len(friends), 0)

        @pl.when(z == at_z)
        def _():
            for friend in friends:
                greet(at_plane(friend))

    for h in range(HEADS):
        for i in (1, 2, 0, 3):
            load(i, h).wait()

    def square(block):
        block = block.astype(F32)
        return block * block

    def squares(h, sums):
        return sums[0] + square(qd[h, 1]), sums[1] + square(kv[h, 1])

    zeros = jnp.zeros((TOKC, HDIM), F32)
    sums = lax.fori_loop(0, HEADS, squares, (zeros, zeros))
    tile[0] = to_rows([jnp.sum(part_sum, axis=1, keepdims=True) for part_sum in sums])
    pl.semaphore_wait(barrier, 16 + degree)

    def reduce_copy(phase, shift):
        return remote(
            tile.at[phase], tiler.at[phase, shift - 1], ars.at[phase, shift - 1], arr.at[phase, shift - 1],
            (c, (g + shift) % HEAD_DEVICES),
        )

    def reduce_start(phase):
        for shift in range(1, HEAD_DEVICES):
            reduce_copy(phase, shift).start()

    def reduce_finish(phase):
        total = tile[phase]
        for shift in range(1, HEAD_DEVICES):
            reduce_copy(phase, shift).wait_recv()
            total = total + tiler[phase, shift - 1]
        return total

    def kv_own(h):
        return remote(kv.at[h], kvr.at[1, h], kvs.at[0, h], kvrs.at[1, h], dev(c + 2))

    def kv_beside(h):
        return remote(kv.at[h], kvr.at[0, h], kvs.at[1, h], kvrs.at[0, h], dev(c + 1))

    def kv_onward(h):
        return remote(kvr.at[1, h], kvr.at[2, h], kvs.at[1, h], kvrs.at[2, h], dev(c + 1))

    def kv_across(h):
        slot = 2 - 2 * par
        return remote(kvr.at[1, h], kvr.at[slot, h], kvs.at[2, h], kvrs.at[slot, h], partner)

    def qd_own(h):
        return remote(qd.at[h], qdr.at[1, h], qds.at[0, h], qdrs.at[1, h], dev(c + STRETCHES - 2))

    def qd_beside(h):
        return remote(qd.at[h], qdr.at[0, h], qds.at[1, h], qdrs.at[0, h], dev(c + STRETCHES - 1))

    def qd_onward(h):
        return remote(qdr.at[1, h], qdr.at[2, h], qds.at[1, h], qdrs.at[2, h], dev(c + STRETCHES - 1))

    def qd_across(h):
        slot = 2 * par
        return remote(qdr.at[1, h], qdr.at[slot, h], qds.at[2, h], qdrs.at[slot, h], partner)

    def kv_arrived(slot, h):
        remote(kvr.at[slot, h], kvr.at[slot, h], kvs.at[0, h], kvrs.at[slot, h], partner).wait_recv()

    def qd_arrived(slot, h):
        remote(qdr.at[slot, h], qdr.at[slot, h], qds.at[0, h], qdrs.at[slot, h], partner).wait_recv()

    def gate(*steps):
        for condition, action in steps:
            pl.when(condition)(lambda act=action: (act(), None)[1])

    kv_has, qd_has = c >= 2, c <= 29
    kv_on = jnp.logical_and(odd, jnp.logical_and(c >= 3, c <= 29))
    qd_on = jnp.logical_and(even, jnp.logical_and(c >= 2, c <= 28))

    def kv_send(h):
        gate((c <= 29, kv_own(h).start), (even, kv_beside(h).start))

    def kv_forward(h):
        gate((kv_has, lambda: kv_arrived(1, h)), (kv_on, kv_onward(h).start), (kv_has, kv_across(h).start))

    def qd_send(h):
        gate((c >= 2, qd_own(h).start), (odd, qd_beside(h).start))

    def qd_forward(h):
        gate((qd_has, lambda: qd_arrived(1, h)), (qd_on, qd_onward(h).start), (qd_has, qd_across(h).start))

    def sink_arrived(s, p, h):
        remote(sinkb.at[s, p, h], sinkb.at[s, p, h], sks.at[0, h], skr.at[s, p, h], partner).wait_recv()

    def chip_copy(h):
        block = sinkb.at[par, part, h]
        return remote(block, block, sks.at[0, h], skr.at[par, part, h], partner)

    def mate_copy(h):
        block = sinkb.at[par, part, h]
        return remote(block, block, sks.at[1, h], skr.at[par, part, h], member(2))

    def relay_copy(h):
        block = sinkb.at[par, y, h]
        return remote(block, block, sks.at[2, h], skr.at[par, y, h], partner)

    def kid_copy(i, kid, h):
        block = sinkb.at[par, part, h]
        return remote(block, block, skc.at[i, h], skr.at[par, part, h], at_plane(kid))

    def value_copy(i, h):
        block = sinkb.at[par, 0, h]
        return remote(block, block, crs.at[i, h], skr.at[par, 0, h], (16 + 2 * VALUE_KIDS[i] + par, g))

    def each_kid(body):
        for column, table in enumerate(KIDS):
            for at_z, kids in table.items():
                @pl.when(jnp.logical_and(y == column, z == at_z))
                def _():
                    for i, kid in enumerate(kids):
                        body(i, kid)

    has_mate = jnp.logical_or(y == 0, z > 0)

    def sink_send(h):
        each_kid(lambda i, kid: kid_copy(i, kid, h).start())
        gate((has_mate, mate_copy(h).start))
        chip_copy(h).start()

    def sink_pass(h):
        @pl.when(jnp.logical_not(owner))
        def _():
            sink_arrived(par, part, h)
            sink_send(h)

    def sink_relay(h):
        @pl.when(jnp.logical_not(owner))
        def _():
            sink_arrived(par, y, h)
            relay_copy(h).start()

    def inverse_copy(stretch):
        return remote(stat_inv, sinv.at[par], svs.at[stretch], svr.at[par], (stretch, g))

    def inverse_arrived(s):
        remote(sinv.at[s], sinv.at[s], svs.at[0], svr.at[s], partner).wait_recv()

    stat_inv = sinv.at[2]

    def each_other(body):
        def at(i, _):
            @pl.when(i != c)
            def _():
                body(i)

            return 0

        lax.fori_loop(0, STRETCHES, at, 0)

    def loop(count, step):
        lax.fori_loop(0, count, lambda h, _: (step(h), 0)[1], 0)

    def launch(h):
        @pl.when(owner)
        def _():
            for p in (0, 1):
                sinkb[par, p, h] = kv[h, p]
            for i in range(len(VALUE_KIDS)):
                value_copy(i, h).start()
            sink_send(h)
            relay_copy(h).start()

        gate((jnp.logical_or(h < AHEAD, jnp.logical_not(paced)), lambda: kv_send(h)))

    def loop_from(low, high, step):
        lax.fori_loop(low, high, lambda h, _: (step(h), 0)[1], 0)

    reduce_start(0)
    loop_from(0, AHEAD, launch)

    for i, hbm in enumerate((query_gain_hbm, key_gain_hbm)):
        load_gain(i, hbm).wait()
    inverse = lax.rsqrt(reduce_finish(0) / D + EPS)
    sinv[2] = inverse

    @pl.when(owner)
    def _():
        sinv[par] = inverse
        each_other(lambda i: inverse_copy(i).start())

    def near_copy(i):
        shift = NEAR[i]
        return remote(sinv.at[2], ninv.at[i], nis.at[i], nir.at[i], dev(c + STRETCHES + shift))

    for i in range(len(NEAR)):
        near_copy(i).start()
    loop_from(AHEAD, HEADS, launch)
    loop(HEADS, lambda h: gate((jnp.logical_not(busy), lambda: qd_send(h))))
    inv[0] = to_full(inverse[0:1])
    inv[1] = to_full(inverse[1:2])

    def gain(i, h):
        return gains[i, pl.ds(pl.multiple_of(h * HDIM, HDIM), HDIM)].reshape(1, HDIM)

    def normed(block, full, i, h):
        return (block.astype(F32) * full * gain(i, h)).astype(BF16)

    def norms(h):
        queryn[h] = normed(qd[h, 1], inv[0], 0, h)
        keyn[h] = normed(kv[h, 1], inv[1], 1, h)

    loop(HEADS, norms)

    far = recent[0, 1]
    sink_id = sink[0, 0]
    far_two = jnp.logical_and(far == c - 2, c >= 2)
    far_three = jnp.logical_and(far == c - 3, c >= 3)
    two = jnp.where(far_two, 1.0, 0.0).astype(F32)
    sink_one = jnp.where(sink_id == 1, 1.0, 0.0).astype(F32)
    sink_zero = jnp.where(sink_id == 0, 1.0, 0.0).astype(F32)
    near_off = jnp.where(c >= 1, 0.0, FAR_AWAY).astype(F32)
    two_off = jnp.where(far_two, 0.0, FAR_AWAY).astype(F32)
    three_off = jnp.where(far_three, 0.0, FAR_AWAY).astype(F32)
    far_off = jnp.minimum(two_off, three_off)
    sink_off = jnp.where(sink_id >= 0, 0.0, FAR_AWAY).astype(F32)

    def blend(first, second, share):
        return first.astype(F32) * share + second.astype(F32) * (1.0 - share)

    def mix(first, second, share):
        return blend(first, second, share).astype(BF16)

    def key_side(keys, vals, queries, grads, log_row, delta_row):
        prob = jnp.exp2(dot_t(keys, queries) * SCALE2 - log_row)
        dprob = dot_t(vals, grads)
        dscore = (prob * (dprob - delta_row)).astype(BF16)
        return dot_n(dscore, queries), dot_n(prob.astype(BF16), grads)

    def stat_copy(shift, h):
        return remote(
            stat.at[h], statr.at[shift - 1, h], sts.at[shift - 1, h], strs.at[shift - 1, h],
            dev(c + STRETCHES - shift),
        )

    def partial_copy(i, h):
        s, p = (par + i % 2) % 2, 1 - (y + i // 2) % 2
        return remote(red.at[s, p, h], rr1.at[i - 1, h], rs1.at[i - 1, h], rr1s.at[i - 1, h], member(i))

    def query_side(h):
        gate((c >= 1, lambda: kv_arrived(0, h)), (c >= 3, lambda: kv_arrived(2, h)))
        for p in (0, 1):
            sink_arrived(1 - par, p, h)

        queries, grads = queryn[h], qd[h, 0]
        sink_raw = blend(sinkb[1, 1, h], sinkb[0, 1, h], sink_one) * gain(1, h)
        sink_keys = (sink_raw * inv[2]).astype(BF16)
        sink_vals = mix(sinkb[1, 0, h], sinkb[0, 0, h], sink_one)
        far_keys = normed(blend(kvr[1, h, 1], kvr[2, h, 1], two), inv[4], 1, h)
        blocks = (
            (keyn[h], kv[h, 0], 0.0),
            (normed(kvr[0, h, 1], inv[3], 1, h), kvr[0, h, 0], near_off),
            (far_keys, mix(kvr[1, h, 0], kvr[2, h, 0], two), far_off),
            (sink_keys, sink_vals, sink_off),
        )
        scores = [dot_t(queries, keys) * SCALE2 for keys, _, _ in blocks]
        top = None
        for score, block in zip(scores, blocks):
            here = jnp.max(score, axis=1, keepdims=True) - block[2]
            top = here if top is None else jnp.maximum(top, here)
        probs = [jnp.exp2(score - (top + block[2])) for score, block in zip(scores, blocks)]
        total = None
        for prob in probs:
            here = jnp.sum(prob, axis=1, keepdims=True)
            total = here if total is None else total + here
        share = 1.0 / total
        attended = jnp.zeros((TOKC, HDIM), F32)
        probs = [prob * share for prob in probs]
        for prob, block in zip(probs, blocks):
            attended = attended + dot_n(prob.astype(BF16), block[1])
        attended = attended.astype(BF16)
        att_out[:, pl.ds(pl.multiple_of(h * HDIM, HDIM), HDIM)] = attended
        delta = jnp.sum(grads.astype(F32) * attended.astype(F32), axis=1, keepdims=True)
        log_total = top + jnp.log2(total)
        rows = to_rows(
            (
                log_total, delta, log_total + near_off, log_total + two_off, log_total + three_off,
                log_total + sink_off,
            )
        )
        stat[h] = rows
        sink_dk, sink_dv = key_side(sink_keys, sink_vals, queries, grads, rows[5:6], rows[1:2])
        tsum[...] = tsum[...] + sink_dk * sink_raw
        for s, mine in ((0, sink_zero), (1, sink_one)):
            red[s, 1, h] = (sink_dk * mine).astype(BF16)
            red[s, 0, h] = (sink_dv * mine).astype(BF16)
        for i in (2, 3, 1):
            partial_copy(i, h).start()
        for shift in (1, 2, 3):
            stat_copy(shift, h).start()

        query_delta = jnp.zeros((TOKC, HDIM), F32)
        for prob, block in zip(probs, blocks):
            dscore = (prob * (dot_t(grads, block[1]) - delta)).astype(BF16)
            query_delta = query_delta + dot_n(dscore, block[0])
        dq[h] = query_delta * SCALE

    def owner_side(h):
        keys, vals = keyn[h], kv[h, 0]
        key_sum, value_sum = key_side(keys, vals, queryn[h], qd[h, 0], stat[h, 0:1], stat[h, 1:2])
        for slot in range(3):
            if slot != 1:
                gate((c <= 30 - slot, lambda: qd_arrived(slot, h)))
            stat_copy(slot + 1, h).wait_recv()
            more_keys, more_values = key_side(
                keys, vals, normed(qdr[slot, h, 1], inv[5 + slot], 0, h), qdr[slot, h, 0],
                statr[slot, h, slot + 2:slot + 3], statr[slot, h, 1:2],
            )
            key_sum, value_sum = key_sum + more_keys, value_sum + more_values
        dk[h] = key_sum
        dv[h] = value_sum

    def up_copy(slot, parent, h):
        return remote(up.at[h], rr2.at[slot, h], rs2.at[h], rr2s.at[slot, h], at_plane(parent))

    def each_parent(body):
        for parent, below in SUMS.items():
            for slot, kid in enumerate(below):
                @pl.when(z == kid)
                def _():
                    body(slot, parent)

    def up_send(h):
        up[h] = acc[h].astype(BF16)
        each_parent(lambda slot, parent: up_copy(slot, parent, h).start())

    def plane_sum(h):
        total = red[par, part, h].astype(F32)
        for slot in range(3):
            remote(rr1.at[slot, h], rr1.at[slot, h], rs1.at[0, h], rr1s.at[slot, h], partner).wait_recv()
            total = total + rr1[slot, h].astype(F32)
        acc[h] = total

        @pl.when(is_leaf)
        def _():
            up_send(h)

    def below_sum(h, count):
        total = acc[h]
        for slot in range(count):
            remote(rr2.at[slot, h], rr2.at[slot, h], rs2.at[h], rr2s.at[slot, h], partner).wait_recv()
            total = total + rr2[slot, h].astype(F32)
        acc[h] = total

    def value_back(h):
        return remote(up.at[h], vin.at[h], vis.at[h], vir.at[h], (par, g))

    is_leaf = z < 0
    for at_z in range(1, 8):
        if at_z not in SUMS:
            is_leaf = jnp.logical_or(is_leaf, z == at_z)

    def when_in(at, low, body):
        @pl.when(jnp.logical_and(at >= low, at < low + HEADS))
        def _():
            body(at - low)

    def middle(h):
        for at_z in SUMS:
            if at_z:
                @pl.when(z == at_z)
                def _():
                    below_sum(h, len(SUMS[at_z]))
                    up_send(h)

    def finish(h):
        below_sum(h, len(SUMS[0]))

        @pl.when(y == 0)
        def _():
            dk[h] = dk[h] + acc[h]

        @pl.when(y == 1)
        def _():
            up[h] = acc[h].astype(BF16)
            value_back(h).start()

    def prepare():
        @pl.when(c != 0)
        def _():
            inverse_arrived(0)

        @pl.when(c != 1)
        def _():
            inverse_arrived(1)

        for i in range(len(NEAR)):
            near_copy(i).wait_recv()
        inv[2] = to_full(sinv[1, 1:2] * sink_one + sinv[0, 1:2] * (1.0 - sink_one))
        inv[3] = to_full(ninv[0, 1:2])
        inv[4] = to_full(ninv[1, 1:2] * two + ninv[2, 1:2] * (1.0 - two))
        for slot in range(3):
            inv[5 + slot] = to_full(ninv[3 + slot, 0:1])

    tsum[...] = jnp.zeros((TOKC, HDIM), F32)

    def step(at):
        when_in(at, 0, kv_forward)
        when_in(at, lag_pass, sink_pass)
        gate((jnp.logical_and(paced, at < HEADS - AHEAD), lambda: kv_send(at + AHEAD)))
        when_in(at, lag_relay, sink_relay)
        when_in(at, lag_pass, lambda h: gate((busy, lambda: qd_send(h))))

        @pl.when(at == lag_query)
        def _():
            prepare()

        when_in(at, lag_query, query_side)
        when_in(at, 4, qd_forward)
        when_in(at, 10, owner_side)
        when_in(at, lag_query + 1, plane_sum)
        when_in(at, 9, middle)

    loop(HEADS + 10, step)

    def tile_copy(root):
        return remote(tout, tin.at[c], tis.at[root], tir.at[c], (root, g))

    sink_inner = jnp.sum(tsum[...], axis=1, keepdims=True) * SCALE
    tout[...] = to_rows((sink_inner * sink_zero, sink_inner * sink_one))
    for root in (0, 1):
        @pl.when(c != root)
        def _():
            tile_copy(root).start()

    def inner(h, sums):
        return (
            sums[0] + dq[h] * (gain(0, h) * qd[h, 1].astype(F32)),
            sums[1] + dk[h] * (gain(1, h) * SCALE * kv[h, 1].astype(F32)),
        )

    sums = lax.fori_loop(0, HEADS, inner, (zeros, zeros))
    tile[1] = to_rows([jnp.sum(part_sum, axis=1, keepdims=True) for part_sum in sums])

    @pl.when(owner)
    def _():
        tin[c] = tout[...]

        def gather(i):
            remote(tin.at[i], tin.at[i], tis.at[0], tir.at[i], partner).wait_recv()
            tin[c] = tin[c] + tin[i]

        each_other(gather)
        sums = tin[c]
        mine = jnp.where(odd, 1.0, 0.0).astype(F32)
        row = sums[0:1] * (1.0 - mine) + sums[1:2] * mine
        level = lax.broadcasted_iota(jnp.int32, (8, TOKC), 0)
        tile[1] = tile[1] + jnp.where(level == 1, row, 0.0)

    reduce_start(1)
    total = reduce_finish(1)
    query_inner = to_full(total[0:1]) * inv[0] * inv[0] * inv[0] / D
    inv[2] = to_full(total[1:2]) * inv[1] * inv[1] * inv[1] / D
    for h in range(HEADS):
        at = pl.ds(h * HDIM, HDIM)
        dq_out[:, at] = (dq[h] * gain(0, h) * inv[0] - qd[h, 1].astype(F32) * query_inner).astype(BF16)

    @pl.when(z == 0)
    def _():
        loop(HEADS, finish)

    for h in range(HEADS):
        at = pl.ds(h * HDIM, HDIM)
        dk_out[:, at] = (dk[h] * SCALE * gain(1, h) * inv[1] - kv[h, 1].astype(F32) * inv[2]).astype(BF16)

    @pl.when(owner)
    def _():
        for h in range(HEADS):
            value_back(h).wait_recv()
            dv[h] = dv[h] + vin[h].astype(F32)

    for h in range(HEADS):
        dv_out[:, pl.ds(h * HDIM, HDIM)] = dv[h].astype(BF16)

    def drain(h):
        gate(
            (c <= 29, kv_own(h).wait_send), (jnp.logical_or(even, kv_on), kv_beside(h).wait_send),
            (kv_has, kv_across(h).wait_send), (c >= 2, qd_own(h).wait_send),
            (jnp.logical_or(odd, qd_on), qd_beside(h).wait_send), (qd_has, qd_across(h).wait_send),
            (has_mate, mate_copy(h).wait_send),
        )
        each_kid(lambda i, kid: kid_copy(i, kid, h).wait_send())
        chip_copy(h).wait_send()
        relay_copy(h).wait_send()
        for i in (1, 2, 3):
            partial_copy(i, h).wait_send()
            stat_copy(i, h).wait_send()
        each_parent(lambda slot, parent: up_copy(slot, parent, h).wait_send())

        @pl.when(owner)
        def _():
            for i in range(len(VALUE_KIDS)):
                value_copy(i, h).wait_send()

        @pl.when(jnp.logical_and(z == 0, y == 1))
        def _():
            value_back(h).wait_send()

    loop(HEADS, drain)

    @pl.when(owner)
    def _():
        each_other(lambda i: inverse_copy(i).wait_send())

    for root in (0, 1):
        @pl.when(c != root)
        def _():
            tile_copy(root).wait_send()

    for i in range(len(NEAR)):
        near_copy(i).wait_send()
    for phase in (0, 1):
        for shift in range(1, HEAD_DEVICES):
            reduce_copy(phase, shift).wait_send()


def per_device(query_raw, key_raw, values, query_gain, key_gain, recent_ids, sink_ids, out_grad):
    rows, width = query_raw.shape
    block = (HEADS, TOKC, HDIM)
    pair = (HEADS, 2, TOKC, HDIM)
    dma = pltpu.SemaphoreType.DMA
    any_spec = pl.BlockSpec(memory_space=pl.ANY)
    vmem = pl.BlockSpec(memory_space=pltpu.VMEM)
    smem = pl.BlockSpec(memory_space=pltpu.SMEM)
    return pl.pallas_call(
        kernel,
        out_shape=[jax.ShapeDtypeStruct((rows, width), BF16)] * 4,
        in_specs=[any_spec] * 6 + [smem] * 2,
        out_specs=[vmem] * 4,
        scratch_shapes=[
            pltpu.VMEM(pair, BF16),
            pltpu.VMEM(pair, BF16),
            pltpu.VMEM(block, BF16),
            pltpu.VMEM(block, BF16),
            pltpu.VMEM((3,) + pair, BF16),
            pltpu.VMEM((3,) + pair, BF16),
            pltpu.VMEM((2, 2) + block, BF16),
            pltpu.VMEM((2, 2) + block, BF16),
            pltpu.VMEM((3,) + block, BF16),
            pltpu.VMEM((3,) + block, BF16),
            pltpu.VMEM(block, F32),
            pltpu.VMEM(block, BF16),
            pltpu.VMEM(block, BF16),
            pltpu.VMEM(block, F32),
            pltpu.VMEM(block, F32),
            pltpu.VMEM(block, F32),
            pltpu.VMEM((HEADS, 8, TOKC), F32),
            pltpu.VMEM((3, HEADS, 8, TOKC), F32),
            pltpu.VMEM((2, 8, TOKC), F32),
            pltpu.VMEM((2, HEAD_DEVICES - 1, 8, TOKC), F32),
            pltpu.VMEM((8, TOKC, HDIM), F32),
            pltpu.VMEM((2, width), F32),
            pltpu.VMEM((3, 8, TOKC), F32),
            pltpu.VMEM((len(NEAR), 8, TOKC), F32),
            pltpu.VMEM((TOKC, HDIM), F32),
            pltpu.VMEM((8, TOKC), F32),
            pltpu.VMEM((STRETCHES, 8, TOKC), F32),
            dma((4, HEADS)),
            dma((2,)),
            dma((3, HEADS)),
            dma((3, HEADS)),
            dma((3, HEADS)),
            dma((3, HEADS)),
            dma((3, HEADS)),
            dma((3, HEADS)),
            dma((2, 2, HEADS)),
            dma((3, HEADS)),
            dma((3, HEADS)),
            dma((2, HEAD_DEVICES - 1)),
            dma((2, HEAD_DEVICES - 1)),
            dma((3, HEADS)),
            dma((3, HEADS)),
            dma((HEADS,)),
            dma((3, HEADS)),
            dma((HEADS,)),
            dma((HEADS,)),
            dma((len(VALUE_KIDS), HEADS)),
            dma((STRETCHES,)),
            dma((2,)),
            dma((2,)),
            dma((STRETCHES,)),
            dma((len(NEAR),)),
            dma((len(NEAR),)),
        ],
        compiler_params=pltpu.CompilerParams(
            collective_id=0, has_side_effects=True, vmem_limit_bytes=60 * 2**20
        ),
        cost_estimate=pl.CostEstimate(flops=3 * 10**9, bytes_accessed=6 * 10**6, transcendentals=3 * 10**6),
        name="stretch_attention",
    )(
        query_raw, key_raw, values, out_grad, query_gain, key_gain, recent_ids, sink_ids,
    )


def solution(mesh):
    split = P("stretch", "head")
    return jax.shard_map(
        per_device,
        mesh=mesh,
        in_specs=(split, split, split, P("head"), P("head"), P("stretch", None), P("stretch", None), split),
        out_specs=(split,) * 4,
        check_vma=False,
    )
```

time: 122 us -> 108 us (0.89)
  Pallas kernels: 112 us -> 102 us
  local copies, waits for them, and re-layouts: 8.14 us -> 4.68 us
    pallas_call x1, Pallas kernels: 112 us -> 102 us  [per_device(): pl.pallas_call(kernel, out_shape=[jax.ShapeDtypeStruct((rows, width), BF1...]
    unnamed x16 -> x10, local copies, waits for them, and re-layouts: 7.44 us -> 4.68 us
where the time goes in v2:
time: 108 us
  Pallas kernels  102 us (94%)
  local copies, waits for them, and re-layouts  4.68 us (4%)
  between operations  1.3 us (1%)
    pallas_call x1, Pallas kernels, per_device(): pl.pallas_call(kernel, out_shape=[jax.ShapeDtypeStruct((rows, width), BF1...  102 us
    unnamed x10, local copies, waits for them, and re-layouts  4.68 us

profile of v2, /device:TPU:1, one launch (start us, length us, event | category | flops | bytes accessed | tf_op | source)
XLA Modules:
  0.0 107.7 jit_solution(9667565985490144970)
XLA Ops:
  1.3 101.7 %stretch_attention.1 = (bf16[256,640]{1,0:T(8,128)(2,1)}, bf16[256,640]{1,0:T(8,128)(2,1)}, bf16[256,640]{1,0:T(8,128)(2,1)}, bf16[256,640]{1,0:T(8,128)(2,1)}) custom-call(bf16[256,640]{1,0:T(8,128)(2,1)} %query_hbm.1, bf16[256,640]{1,0:T(8,128)(2,1)} %key_hbm.1, bf16[256,640]{1,0:T(8,128)(2,1)} %values_hbm.1, bf16[256,640]{1,0:T(8,128)(2,1)} %grad_hbm.1, ...), custom_call_target="tpu_custom_call" | custom-call | flops 3000000000 | bytes 6000000 | tf_op jit(solution)/shard_map/stretch_attention/pallas_call | solution.py:676
  103.0 0.0 copy-start.2
  103.0 1.8 %copy.17 = bf16[256,640]{1,0:T(8,128)(2,1)} copy(bf16[256,640]{1,0:T(8,128)(2,1)} %get-tuple-element.8) | data formatting | bytes 655360
  104.7 0.0 copy-done.2
  104.7 0.0 copy-start.1
  104.7 0.7 copy.18
  105.5 0.4 copy-done.1
  105.8 0.0 copy-start
  105.8 0.7 copy.19
  106.6 0.4 copy-done
  106.9 0.7 copy.20
Async XLA Ops:
  103.0 1.8 %copy-start.2 = (bf16[256,640]{1,0:T(8,128)(2,1)S(1)}, bf16[256,640]{1,0:T(8,128)(2,1)}, u32[]{:S(2)}) copy-start(bf16[256,640]{1,0:T(8,128)(2,1)} %get-tuple-element.9) | copy-start | bytes 983044
  104.7 1.1 %copy-start.1 = (bf16[256,640]{1,0:T(8,128)(2,1)S(1)}, bf16[256,640]{1,0:T(8,128)(2,1)}, u32[]{:S(2)}) copy-start(bf16[256,640]{1,0:T(8,128)(2,1)} %get-tuple-element.10) | copy-start | bytes 983044
  105.8 1.1 %copy-start = (bf16[256,640]{1,0:T(8,128)(2,1)S(1)}, bf16[256,640]{1,0:T(8,128)(2,1)}, u32[]{:S(2)}) copy-start(bf16[256,640]{1,0:T(8,128)(2,1)} %get-tuple-element.11) | copy-start | bytes 983044

commit v3 on v2

--- a/solution.py
+++ b/solution.py
@@ -19,7 +19,7 @@
 NEAR = (1, 2, 3, -1, -2, -3)
 KIDS = ({0: (1, 7), 1: (2,), 7: (6, 5), 5: (4, 3)}, {1: (2,), 7: (6, 5, 0), 5: (4, 3)})
 VALUE_KIDS = (1, 7)
-AHEAD = 2
+AHEAD = 3
 SUMS = {0: (1, 7, 5), 1: (2,), 7: (6,), 5: (4, 3)}
 F32 = jnp.float32
 BF16 = jnp.bfloat16
@@ -85,6 +85,7 @@
     lag_query = jnp.where(owner, 2, 2 * level + 1)
     paced = z == 1
     busy = (z == 7) | (z == 5)
+    lag_owner = jnp.where(level == 3, 11, 9)
 
     def load(i, h):
         hbm, dst, p = loads[i]
@@ -313,6 +314,7 @@
             relay_copy(h).start()
 
         gate((jnp.logical_or(h < AHEAD, jnp.logical_not(paced)), lambda: kv_send(h)))
+        gate((jnp.logical_not(busy), lambda: qd_send(h)))
 
     def loop_from(low, high, step):
         lax.fori_loop(low, high, lambda h, _: (step(h), 0)[1], 0)
@@ -337,7 +339,6 @@
     for i in range(len(NEAR)):
         near_copy(i).start()
     loop_from(AHEAD, HEADS, launch)
-    loop(HEADS, lambda h: gate((jnp.logical_not(busy), lambda: qd_send(h))))
     inv[0] = to_full(inverse[0:1])
     inv[1] = to_full(inverse[1:2])
 
@@ -545,6 +546,17 @@
 
     tsum[...] = jnp.zeros((TOKC, HDIM), F32)
 
+    def tile_copy(root):
+        return remote(tout, tin.at[c], tis.at[root], tir.at[c], (root, g))
+
+    def tile_send():
+        sink_inner = jnp.sum(tsum[...], axis=1, keepdims=True) * SCALE
+        tout[...] = to_rows((sink_inner * sink_zero, sink_inner * sink_one))
+        for root in (0, 1):
+            @pl.when(c != root)
+            def _():
+                tile_copy(root).start()
+
     def step(at):
         when_in(at, 0, kv_forward)
         when_in(at, lag_pass, sink_pass)
@@ -557,22 +569,13 @@
             prepare()
 
         when_in(at, lag_query, query_side)
-        when_in(at, 4, qd_forward)
-        when_in(at, 10, owner_side)
+        gate((at == lag_query + HEADS - 1, tile_send))
         when_in(at, lag_query + 1, plane_sum)
         when_in(at, 9, middle)
-
-    loop(HEADS + 10, step)
-
-    def tile_copy(root):
-        return remote(tout, tin.at[c], tis.at[root], tir.at[c], (root, g))
-
-    sink_inner = jnp.sum(tsum[...], axis=1, keepdims=True) * SCALE
-    tout[...] = to_rows((sink_inner * sink_zero, sink_inner * sink_one))
-    for root in (0, 1):
-        @pl.when(c != root)
-        def _():
-            tile_copy(root).start()
+        when_in(at, 7, qd_forward)
+        when_in(at, lag_owner, owner_side)
+
+    loop(HEADS + 11, step)
 
     def inner(h, sums):
         return (
@@ -599,6 +602,7 @@
         tile[1] = tile[1] + jnp.where(level == 1, row, 0.0)
 
     reduce_start(1)
+    gate((jnp.logical_and(z == 0, y == 1), lambda: loop(HEADS, finish)))
     total = reduce_finish(1)
     query_inner = to_full(total[0:1]) * inv[0] * inv[0] * inv[0] / D
     inv[2] = to_full(total[1:2]) * inv[1] * inv[1] * inv[1] / D
@@ -606,9 +610,7 @@
         at = pl.ds(h * HDIM, HDIM)
         dq_out[:, at] = (dq[h] * gain(0, h) * inv[0] - qd[h, 1].astype(F32) * query_inner).astype(BF16)
 
-    @pl.when(z == 0)
-    def _():
-        loop(HEADS, finish)
+    gate((owner, lambda: loop(HEADS, finish)))
 
     for h in range(HEADS):
         at = pl.ds(h * HDIM, HDIM)
@@ -665,15 +667,28 @@
             reduce_copy(phase, shift).wait_send()
 
 
+def hand_on(*refs):
+    held, sem = refs[8:]
+    reads = [pltpu.make_async_copy(refs[i], held.at[i], sem.at[0, i]) for i in range(4)]
+    writes = [pltpu.make_async_copy(held.at[i], refs[4 + i], sem.at[1, i]) for i in range(4)]
+    for read in reads:
+        read.start()
+    for read, write in zip(reads, writes):
+        read.wait()
+        write.start()
+    for write in writes:
+        write.wait()
+
+
 def per_device(query_raw, key_raw, values, query_gain, key_gain, recent_ids, sink_ids, out_grad):
     rows, width = query_raw.shape
     block = (HEADS, TOKC, HDIM)
     pair = (HEADS, 2, TOKC, HDIM)
     dma = pltpu.SemaphoreType.DMA
-    any_spec = pl.BlockSpec(memory_space=pl.ANY)
+    any_spec = pl.BlockSpec(memory_space=pltpu.HBM)
     vmem = pl.BlockSpec(memory_space=pltpu.VMEM)
     smem = pl.BlockSpec(memory_space=pltpu.SMEM)
-    return pl.pallas_call(
+    outputs = pl.pallas_call(
         kernel,
         out_shape=[jax.ShapeDtypeStruct((rows, width), BF16)] * 4,
         in_specs=[any_spec] * 6 + [smem] * 2,
@@ -741,6 +756,14 @@
     )(
         query_raw, key_raw, values, out_grad, query_gain, key_gain, recent_ids, sink_ids,
     )
+    return pl.pallas_call(
+        hand_on,
+        out_shape=[jax.ShapeDtypeStruct((rows, width), BF16)] * 4,
+        in_specs=[any_spec] * 4,
+        out_specs=[any_spec] * 4,
+        scratch_shapes=[pltpu.VMEM((4, rows, width), BF16), dma((2, 4))],
+        name="hand_on",
+    )(*outputs)
 
 
 def solution(mesh):

time: 108 us -> 90.9 us (0.84)
  Pallas kernels: 102 us -> 89.4 us
  local copies, waits for them, and re-layouts: 4.68 us -> 0 us
    pallas_call x1, Pallas kernels: 102 us -> 87.3 us  [per_device(): pl.pallas_call(kernel, out_shape=[jax.ShapeDtypeStruct((rows, width), BF1...]
    unnamed x10 -> x0, local copies, waits for them, and re-layouts: 4.68 us -> none
    pallas_call x0 -> x1, Pallas kernels: none -> 2.09 us  [per_device(): pl.pallas_call(hand_on, out_shape=[jax.ShapeDtypeStruct((rows, width), BF...]
where the time goes in v3:
time: 90.9 us; the launch traced here: 90.7 us
  Pallas kernels  89.4 us (98%)
  between operations  1.29 us (1%)
    pallas_call x1, Pallas kernels, per_device(): pl.pallas_call(kernel, out_shape=[jax.ShapeDtypeStruct((rows, width), BF1...  87.3 us
    pallas_call x1, Pallas kernels, per_device(): pl.pallas_call(hand_on, out_shape=[jax.ShapeDtypeStruct((rows, width), BF...  2.09 us

profile of v3, /device:TPU:1, one launch (start us, length us, event | category | flops | bytes accessed | tf_op | source)
XLA Modules:
  0.0 90.7 jit_solution(17922571134585470699)
XLA Ops:
  1.3 87.3 %stretch_attention.1 = (bf16[256,640]{1,0:T(8,128)(2,1)}, bf16[256,640]{1,0:T(8,128)(2,1)}, bf16[256,640]{1,0:T(8,128)(2,1)}, bf16[256,640]{1,0:T(8,128)(2,1)}) custom-call(bf16[256,640]{1,0:T(8,128)(2,1)} %query_hbm.1, bf16[256,640]{1,0:T(8,128)(2,1)} %key_hbm.1, bf16[256,640]{1,0:T(8,128)(2,1)} %values_hbm.1, bf16[256,640]{1,0:T(8,128)(2,1)} %grad_hbm.1, ...), custom_call_target="tpu_custom_call" | custom-call | flops 3000000000 | bytes 6000000 | tf_op jit(solution)/shard_map/stretch_attention/pallas_call | solution.py:691
  88.6 2.1 %hand_on.1 = (bf16[256,640]{1,0:T(8,128)(2,1)}, bf16[256,640]{1,0:T(8,128)(2,1)}, bf16[256,640]{1,0:T(8,128)(2,1)}, bf16[256,640]{1,0:T(8,128)(2,1)}) custom-call(bf16[256,640]{1,0:T(8,128)(2,1)} %get-tuple-element.8.refs_0_, bf16[256,640]{1,0:T(8,128)(2,1)} %get-tuple-element.9.refs_1_, bf16[256,640]{1,0:T(8,128)(2,1)} %get-tuple-element.10.refs_2_, ...), custom_call_target="tpu_custom_call" | custom-call | tf_op jit(solution)/shard_map/hand_on/pallas_call | solution.py:759

commit v4 on v3

--- a/solution.py
+++ b/solution.py
@@ -19,7 +19,7 @@
 NEAR = (1, 2, 3, -1, -2, -3)
 KIDS = ({0: (1, 7), 1: (2,), 7: (6, 5), 5: (4, 3)}, {1: (2,), 7: (6, 5, 0), 5: (4, 3)})
 VALUE_KIDS = (1, 7)
-AHEAD = 3
+AHEAD = 4
 SUMS = {0: (1, 7, 5), 1: (2,), 7: (6,), 5: (4, 3)}
 F32 = jnp.float32
 BF16 = jnp.bfloat16
@@ -84,7 +84,7 @@
     lag_relay = 2 * level
     lag_query = jnp.where(owner, 2, 2 * level + 1)
     paced = z == 1
-    busy = (z == 7) | (z == 5)
+    busy = z >= 4
     lag_owner = jnp.where(level == 3, 11, 9)
 
     def load(i, h):
@@ -562,7 +562,7 @@
         when_in(at, lag_pass, sink_pass)
         gate((jnp.logical_and(paced, at < HEADS - AHEAD), lambda: kv_send(at + AHEAD)))
         when_in(at, lag_relay, sink_relay)
-        when_in(at, lag_pass, lambda h: gate((busy, lambda: qd_send(h))))
+        when_in(at, 1, lambda h: gate((busy, lambda: qd_send(h))))
 
         @pl.when(at == lag_query)
         def _():

time: 90.9 us -> 90.6 us (level)
  no operation moved by 1% of the time
where the time goes in v4:
time: 90.6 us; the launch traced here: 90.4 us
  Pallas kernels  89.1 us (98%)
  between operations  1.29 us (1%)
    pallas_call x1, Pallas kernels, per_device(): pl.pallas_call(kernel, out_shape=[jax.ShapeDtypeStruct((rows, width), BF1...  87 us
    pallas_call x1, Pallas kernels, per_device(): pl.pallas_call(hand_on, out_shape=[jax.ShapeDtypeStruct((rows, width), BF...  2.09 us

profile of v4, /device:TPU:1, one launch (start us, length us, event | category | flops | bytes accessed | tf_op | source)
XLA Modules:
  0.0 90.4 jit_solution(13826655575245183244)
XLA Ops:
  1.3 87.0 %stretch_attention.1 = (bf16[256,640]{1,0:T(8,128)(2,1)}, bf16[256,640]{1,0:T(8,128)(2,1)}, bf16[256,640]{1,0:T(8,128)(2,1)}, bf16[256,640]{1,0:T(8,128)(2,1)}) custom-call(bf16[256,640]{1,0:T(8,128)(2,1)} %query_hbm.1, bf16[256,640]{1,0:T(8,128)(2,1)} %key_hbm.1, bf16[256,640]{1,0:T(8,128)(2,1)} %values_hbm.1, bf16[256,640]{1,0:T(8,128)(2,1)} %grad_hbm.1, ...), custom_call_target="tpu_custom_call" | custom-call | flops 3000000000 | bytes 6000000 | tf_op jit(solution)/shard_map/stretch_attention/pallas_call | solution.py:691
  88.3 2.1 %hand_on.1 = (bf16[256,640]{1,0:T(8,128)(2,1)}, bf16[256,640]{1,0:T(8,128)(2,1)}, bf16[256,640]{1,0:T(8,128)(2,1)}, bf16[256,640]{1,0:T(8,128)(2,1)}) custom-call(bf16[256,640]{1,0:T(8,128)(2,1)} %get-tuple-element.8.refs_0_, bf16[256,640]{1,0:T(8,128)(2,1)} %get-tuple-element.9.refs_1_, bf16[256,640]{1,0:T(8,128)(2,1)} %get-tuple-element.10.refs_2_, ...), custom_call_target="tpu_custom_call" | custom-call | tf_op jit(solution)/shard_map/hand_on/pallas_call | solution.py:759
